TPU v7x, 32 devices: a whole 2x2x4 slice. The times are simulated.
32 devices in a mesh: groups: 2 (over y), tensor: 4 (over x, core), dp: 4 (over z).
Axes of the slice: x: 2, y: 2, z: 4, core: 2. Of those that a mesh axis runs over, the one named last changes fastest.
Arguments:
- activations: bfloat16 [16384, 28672], P(('groups', 'dp'), 'tensor'), parts along dimension 0, may hold values from -6 to 6
- out_grads: bfloat16 [16384, 8192], P(('groups', 'dp'), 'tensor'), parts along dimension 0, may hold values from -6 to 6
- proj_in: bfloat16 [57344, 32], P(('groups', 'tensor')), parts along dimension 0, may hold values from -0.03125 to 0.03125
- proj_out: bfloat16 [16384, 32], P(('groups', 'tensor')), parts along dimension 0, may hold values from -0.0625 to 0.0625
- document_ids: int32 [8, 2048], P(('groups', 'dp')), parts along dimension 0, may hold values from 0 to 31, never falling along the last dimension, each value on 1 to 128 neighbouring positions
Outputs:
- sketches: float32 [256, 1024], P(('groups', 'dp'), 'tensor'), parts along dimension 0
- fisher: float32 [2048, 1024], P(('groups', 'dp'), 'tensor'), parts along dimension 0
There are 2 independent parts, one for each index of `groups`. A program takes and returns all parts, laid end to end along the dimension named above; each array names one. Nothing has to cross between parts.
Inputs may be any that keep to these rules, and one draw needn't show every extreme that they name: `document_ids`: each row never falls; each of its 32 documents has 1 to 128 tokens, one exactly 128.
All inputs are finite; a program needn't handle non-finite values.
Results may differ from a plain program's by a relative error of at most 0.0003.
Values sent between devices are 32-bit elements; how exact they have to be, the bound alone decides.
A program may use at most 128 MiB of HBM per device.

v0:
```python
import jax
import jax.numpy as jnp
from jax import lax
from jax.sharding import PartitionSpec as P

DOCS_DEV = 32


def sketch_terms(in_proj, out_proj, weighted):
    token_count = in_proj.shape[0]
    rank_size = in_proj.shape[1]
    outer_rows = (out_proj[:, :, None] * in_proj[:, None, :]).reshape(
        token_count, rank_size * rank_size
    )
    return jnp.dot(weighted.T, outer_rows, precision=lax.Precision.HIGHEST)


def per_device(activations, out_grads, proj_in, proj_out, document_ids):
    in_part = jnp.dot(activations, proj_in, preferred_element_type=jnp.float32)
    out_part = jnp.dot(out_grads, proj_out, preferred_element_type=jnp.float32)
    doc_local = document_ids.shape[0] * 0 + DOCS_DEV
    onehot = (document_ids[0][:, None] == jnp.arange(doc_local, dtype=jnp.int32)[None, :]).astype(
        jnp.float32
    )
    length = jnp.sum(onehot, axis=0)
    weighted = onehot * lax.rsqrt(length)[None, :]
    tensor_count = lax.axis_size("tensor")
    tensor_index = lax.axis_index("tensor")
    sketch_size = proj_in.shape[1] * proj_in.shape[1]
    col_count = sketch_size // tensor_count
    in_proj, out_proj = lax.psum((in_part, out_part), "tensor")
    full_sketch = sketch_terms(in_proj, out_proj, weighted)
    own_sketch = lax.dynamic_slice_in_dim(full_sketch, tensor_index * col_count, col_count, 1)
    dp_count = lax.axis_size("dp")
    total_docs = doc_local * dp_count
    block_rows = sketch_size // dp_count
    row_first = lax.axis_index("dp") * block_rows
    rows_piece = lax.dynamic_slice_in_dim(
        lax.all_gather(full_sketch, "dp", axis=0, tiled=True), row_first, block_rows, 1
    )
    fisher = (
        jnp.dot(
            rows_piece.T,
            lax.all_gather(own_sketch, "dp", axis=0, tiled=True),
            precision=lax.Precision.HIGHEST,
        )
        / total_docs
    )
    return (own_sketch, fisher)


def solution(mesh):
    return jax.shard_map(
        per_device,
        mesh=mesh,
        in_specs=(
            P(("groups", "dp"), "tensor"),
            P(("groups", "dp"), "tensor"),
            P(("groups", "tensor"), None),
            P(("groups", "tensor"), None),
            P(("groups", "dp"), None),
        ),
        out_specs=(P(("groups", "dp"), "tensor"), P(("groups", "dp"), "tensor")),
        check_vma=False,
    )
```

profile of v0, /device:TPU:0, one launch (start us, length us, event | category | flops | bytes accessed | tf_op | source)
XLA Modules:
  0.0 108.7 jit_solution(11769305642774281661)
XLA Ops:
  7.2 0.0 copy-start
  7.2 0.0 copy-start.2
  7.2 0.0 all-reduce.3.cloned.1.call-start
  7.2 1.0 copy-done
  8.2 0.0 copy-start.1
  8.2 14.7 %fusion.9 = f32[2048,32]{0,1:T(8,128)} fusion(bf16[2048,7168]{1,0:T(8,128)(2,1)} %param.5, bf16[7168,32]{0,1:T(8,128)(2,1)S(1)} %copy-done), kind=kOutput, calls=%fused_computation.14 | convolution fusion | flops 939524096 | bytes 30081024 | tf_op jit(solution)/shard_map/dot_general | solution.py:19
  22.9 0.0 copy-done.2
  22.9 0.0 copy-done.1
  22.9 0.0 copy-start.4
  22.9 3.3 %fusion.8 = f32[2048,32]{0,1:T(8,128)} fusion(bf16[2048,2048]{1,0:T(8,128)(2,1)S(1)} %copy-done.1, bf16[2048,32]{0,1:T(8,128)(2,1)S(1)} %copy-done.2), kind=kOutput, calls=%fused_computation.13 | convolution fusion | flops 268435456 | bytes 8781824 | tf_op jit(solution)/shard_map/dot_general | solution.py:20
  26.2 0.0 all-reduce.3.cloned.1.call-update
  26.3 0.0 copy-done.4
  26.3 0.1 convert_reduce_fusion
  26.4 35.9 %all-reduce.3.cloned.1.call-done = (f32[2048,32]{0,1:T(8,128)}, f32[2048,32]{0,1:T(8,128)}) async-done(((f32[2048,32]{0,1:T(8,128)}, f32[2048,32]{0,1:T(8,128)}), (f32[2048,32]{0,1:T(8,128)}, f32[2048,32]{0,1:T(8,128)})) %all-reduce.3.cloned.1.call-update) | async-done | bytes 524304 | tf_op jit(solution)/shard_map/psum | solution.py:31
  62.3 2.1 %broadcast_multiply_fusion = f32[2048,32,32]{0,2,1:T(8,128)S(1)} fusion(f32[2048,32]{0,1:T(8,128)} %get-tuple-element.2, f32[2048,32]{0,1:T(8,128)} %get-tuple-element.3), kind=kLoop, calls=%fused_computation | loop fusion | flops 2097152 | bytes 8912896 | tf_op jit(solution)/shard_map/mul | solution.py:12
  64.4 7.8 %fusion = f32[32,1024]{1,0:T(8,128)S(1)} fusion(f32[2048,1024]{0,1:T(8,128)S(1)} %bitcast.8, f32[32]{0:T(128)S(1)} %rsqrt.7, s32[2048]{0:T(1024)S(1)} %bitcast.10), kind=kOutput, calls=%fused_computation.2 | convolution fusion | flops 805437440 | bytes 8528000 | tf_op jit(solution)/shard_map/dot_general | solution.py:15
  72.2 14.9 %all_gather.6 = f32[128,1024]{1,0:T(8,128)S(1)} all-gather(f32[32,1024]{1,0:T(8,128)S(1)} %fusion), channel_id=1, replica_groups=mesh['groups'=2,'tensor'=4,'dp'=4] {'dp'}, dimensions={0}, use_global_device_ids=true | all-gather | bytes 655360 | tf_op jit(solution)/shard_map/all_gather | solution.py:39
  87.1 0.0 copy-start.3
  87.1 13.7 %all_gather.7 = f32[128,256]{1,0:T(8,128)S(1)} all-gather(f32[32,256]{1,0:T(8,128)S(1)} %constant_dynamic-slice_fusion), channel_id=1, replica_groups=mesh['groups'=2,'tensor'=4,'dp'=4] {'dp'}, dimensions={0}, use_global_device_ids=true | all-gather | bytes 163840 | tf_op jit(solution)/shard_map/all_gather | solution.py:44
  100.8 1.1 %convolution_multiply_fusion = f32[256,256]{1,0:T(8,128)} fusion(f32[128,256]{1,0:T(8,128)S(1)} %all_gather.7, f32[128,1024]{1,0:T(8,128)S(1)} %all_gather.6, s32[]{:T(128)S(6)} %select_n.7), kind=kOutput, calls=%fused_computation.1 | convolution fusion | flops 100728832 | bytes 524292 | tf_op jit(solution)/shard_map/dot_general | solution.py:42
  101.9 0.0 copy-done.3
  (2 shorter events, 0.0 us)
Async XLA Ops:
  7.2 1.0 copy-start
  7.2 15.8 %copy-start.2 = (bf16[2048,32]{0,1:T(8,128)(2,1)S(1)}, bf16[2048,32]{0,1:T(8,128)(2,1)}, u32[]{:S(2)}) copy-start(bf16[2048,32]{0,1:T(8,128)(2,1)} %param.8) | copy-start | bytes 393220
  7.2 55.1 %all-reduce.3.cloned.1.call-start = ((), (), s32[]{:S(2)}) async-start(), calls=%async_computation | async-start | bytes 1048576 | tf_op jit(solution)/shard_map/psum | solution.py:31
  8.2 14.7 %copy-start.1 = (bf16[2048,2048]{1,0:T(8,128)(2,1)S(1)}, bf16[2048,2048]{1,0:T(8,128)(2,1)}, u32[]{:S(2)}) copy-start(bf16[2048,2048]{1,0:T(8,128)(2,1)} %param.6) | copy-start | bytes 25165828
  22.9 3.3 %copy-start.4 = (s32[1,2048]{1,0:T(1,128)S(1)}, s32[1,2048]{1,0:T(1,128)}, u32[]{:S(2)}) copy-start(s32[1,2048]{1,0:T(1,128)} %param.9) | copy-start | bytes 24580
  87.1 14.8 %copy-start.3 = (f32[32,256]{1,0:T(8,128)}, f32[32,256]{1,0:T(8,128)S(1)}, u32[]{:S(2)}) copy-start(f32[32,256]{1,0:T(8,128)S(1)} %constant_dynamic-slice_fusion) | copy-start | bytes 98308
Sparse Core Ops, SparseCore 0:
  26.4 35.9 all-reduce.2
where the time goes:
time: 109 us
  waiting for transfers between devices  35.9 us (33%)
  blocking collectives  28.5 us (26%)
  matrix products  27 us (25%)
  between operations  14.1 us (13%)
  other arithmetic  2.2 us (2%)
    psum x1, waiting for transfers between devices, per_device(): in_proj, out_proj = lax.psum((in_part, out_part), 'tensor')  35.9 us
    all_gather x1, blocking collectives, per_device(): lax.all_gather(full_sketch, 'dp', axis=0, tiled=True)  14.9 us
    dot_general x1, matrix products, per_device(): in_part = jnp.dot(activations, proj_in, preferred_element_type=jnp.float32)  14.7 us
    all_gather x1, blocking collectives, per_device(): lax.all_gather(own_sketch, 'dp', axis=0, tiled=True)  13.7 us
    dot_general x1, matrix products, sketch_terms(): return jnp.dot(weighted.T, outer_rows, precision=lax.Precision.HIGHEST)  7.82 us
    dot_general x1, matrix products, per_device(): out_part = jnp.dot(out_grads, proj_out, preferred_element_type=jnp.float32)  3.29 us
  transfers between devices with their start and end apart: 1, of which 1 were waited for; matrix products, arithmetic and copies ran while one was open for 0% of the time, Pallas kernels for 0%

commit v1 on v0

v1 whole, which is shorter than its diff:
```python
import jax
import jax.numpy as jnp
from jax import lax
from jax.experimental import pallas as pl
from jax.experimental.pallas import tpu as pltpu
from jax.sharding import PartitionSpec as P

DOCS_DEV = 32
MESH = pl.DeviceIdType.MESH
F32 = jnp.float32
BF16 = jnp.bfloat16


def sketch_terms(in_proj, out_proj, weighted):
    token_count = in_proj.shape[0]
    rank_size = in_proj.shape[1]
    outer_rows = (out_proj[:, :, None] * in_proj[:, None, :]).reshape(
        token_count, rank_size * rank_size
    )
    return jnp.dot(weighted.T, outer_rows, precision=lax.Precision.HIGHEST)


def per_device_general(activations, out_grads, proj_in, proj_out, document_ids):
    in_part = jnp.dot(activations, proj_in, preferred_element_type=F32)
    out_part = jnp.dot(out_grads, proj_out, preferred_element_type=F32)
    onehot = (document_ids[0][:, None] == jnp.arange(DOCS_DEV, dtype=jnp.int32)[None, :]).astype(F32)
    length = jnp.sum(onehot, axis=0)
    weighted = onehot * lax.rsqrt(length)[None, :]
    tensor_count = lax.axis_size("tensor")
    tensor_index = lax.axis_index("tensor")
    sketch_size = proj_in.shape[1] * proj_in.shape[1]
    col_count = sketch_size // tensor_count
    in_proj, out_proj = lax.psum((in_part, out_part), "tensor")
    full_sketch = sketch_terms(in_proj, out_proj, weighted)
    own_sketch = lax.dynamic_slice_in_dim(full_sketch, tensor_index * col_count, col_count, 1)
    dp_count = lax.axis_size("dp")
    block_rows = sketch_size // dp_count
    row_first = lax.axis_index("dp") * block_rows
    rows_piece = lax.dynamic_slice_in_dim(
        lax.all_gather(full_sketch, "dp", axis=0, tiled=True), row_first, block_rows, 1
    )
    cols_piece = lax.all_gather(own_sketch, "dp", axis=0, tiled=True)
    fisher = jnp.dot(rows_piece.T, cols_piece, precision=lax.Precision.HIGHEST)
    return (own_sketch, fisher / (DOCS_DEV * dp_count))


N = 4
TB = 256
RANK = 32
OWN = RANK // N


def split(x):
    hi = x.astype(BF16)
    return hi, (x - hi.astype(F32)).astype(BF16)


def kernel(
    act_hbm, grad_hbm, pin_ref, pout_ref, ids_ref, sketch_ref, fisher_ref,
    act, grad, part, sib, mine, send, recv, acc, scol, srow,
    act_sem, grad_sem, sib_send, sib_recv, x_send, x_recv,
    col_send, col_recv, row_send, row_recv,
):
    q = lax.axis_index("tensor")
    z = lax.axis_index("dp")
    blocks = act.shape[0]
    core_peer = q + 1 - 2 * lax.rem(q, 2)
    chip_peer = lax.rem(q + 2, N)

    def load(b):
        rows = pl.ds(pl.multiple_of(b * TB, TB), TB)
        return (
            pltpu.make_async_copy(act_hbm.at[rows], act.at[b], act_sem.at[b]),
            pltpu.make_async_copy(grad_hbm.at[rows], grad.at[b], grad_sem.at[b]),
        )

    def to_core(b):
        return pltpu.make_async_remote_copy(
            src_ref=part.at[b], dst_ref=sib.at[b], send_sem=sib_send.at[b], recv_sem=sib_recv.at[b],
            device_id={"tensor": core_peer}, device_id_type=MESH,
        )

    def to_chip(b):
        return pltpu.make_async_remote_copy(
            src_ref=send.at[b], dst_ref=recv.at[b], send_sem=x_send.at[b], recv_sem=x_recv.at[b],
            device_id={"tensor": chip_peer}, device_id_type=MESH,
        )

    @pl.loop(0, blocks)
    def _(b):
        for copy in load(b):
            copy.start()

    barrier = pltpu.get_barrier_semaphore()
    for dq in range(N):
        for dz in range(N):
            if dq or dz:
                pl.semaphore_signal(
                    barrier, inc=1,
                    device_id={"tensor": lax.rem(q + dq, N), "dp": lax.rem(z + dz, N)},
                    device_id_type=MESH,
                )

    acc[...] = jnp.zeros_like(acc)
    docs = lax.broadcasted_iota(jnp.int32, (DOCS_DEV, 1), 0)
    length = jnp.zeros((DOCS_DEV, 1), F32)
    for b in range(blocks):
        same = (ids_ref[b] == docs).astype(F32)
        length = length + jnp.sum(same, axis=1, keepdims=True)
    scale = lax.rsqrt(length)
    pl.semaphore_wait(barrier, N * N - 1)

    def project(b):
        for copy in load(b):
            copy.wait()
        p_in = jnp.dot(act[b], pin_ref[...], preferred_element_type=F32)
        p_out = jnp.dot(grad[b], pout_ref[...], preferred_element_type=F32)
        part[b, pl.ds(0, RANK)] = p_in.T
        part[b, pl.ds(RANK, RANK)] = p_out.T
        to_core(b).start()

    def chip_sum(b):
        to_core(b).wait()
        total = part[b, pl.ds(0, RANK)] + sib[b, pl.ds(0, RANK)]
        mine[b, pl.ds(0, RANK)] = total
        send[b, pl.ds(0, RANK)] = total
        here = pl.ds(pl.multiple_of(RANK + q * OWN, OWN), OWN)
        there = pl.ds(pl.multiple_of(RANK + chip_peer * OWN, OWN), OWN)
        mine[b, pl.ds(RANK, OWN)] = part[b, here] + sib[b, here]
        send[b, pl.ds(RANK, OWN)] = part[b, there] + sib[b, there]
        to_chip(b).start()

    def sketch(b):
        to_chip(b).wait()
        total = mine[b] + recv[b]
        in_hi, in_lo = split(total[:RANK])
        rhs = jnp.concatenate([in_hi, in_lo], axis=0)
        same = (ids_ref[b] == docs).astype(F32)
        out = total[RANK:]
        out_hi = out.astype(BF16).astype(F32)
        out_lo = out - out_hi
        rows = [same * o[i : i + 1] for o in (out_hi, out_lo) for i in range(OWN)]
        lhs = jnp.concatenate(rows, axis=0).astype(BF16)
        acc[...] += lax.dot_general(
            lhs, rhs, (((1,), (1,)), ((), ())), preferred_element_type=F32
        )

    project(0)
    project(1)
    chip_sum(0)

    @pl.loop(2, blocks)
    def _(b):
        project(b)
        chip_sum(b - 1)
        sketch(b - 2)

    chip_sum(blocks - 1)
    sketch(blocks - 2)
    sketch(blocks - 1)

    half = OWN * DOCS_DEV
    for i in range(OWN):
        hi = acc[pl.ds(i * DOCS_DEV, DOCS_DEV)]
        lo = acc[pl.ds(half + i * DOCS_DEV, DOCS_DEV)]
        both = hi + lo
        piece = (both[:, :RANK] + both[:, RANK:]) * scale
        scol[z, :, pl.ds(i * RANK, RANK)] = piece

    def col_copy(d):
        return pltpu.make_async_remote_copy(
            src_ref=scol.at[z], dst_ref=scol.at[z], send_sem=col_send.at[d], recv_sem=col_recv.at[d],
            device_id={"dp": lax.rem(z + d + 1, N)}, device_id_type=MESH,
        )

    def row_copy(d):
        return pltpu.make_async_remote_copy(
            src_ref=scol.at[z], dst_ref=srow.at[z], send_sem=row_send.at[d], recv_sem=row_recv.at[z],
            device_id={"tensor": lax.rem(q + d + 1, N), "dp": q}, device_id_type=MESH,
        )

    for d in range(N - 1):
        row_copy(d).start()
        col_copy(d).start()
    sketch_ref[...] = scol[z]
    for d in range(N - 1):
        pltpu.make_async_remote_copy(
            src_ref=scol.at[z], dst_ref=scol.at[lax.rem(z + N - d - 1, N)],
            send_sem=col_send.at[d], recv_sem=col_recv.at[d],
            device_id={"dp": lax.rem(z + d + 1, N)}, device_id_type=MESH,
        ).wait_recv()

    @pl.when(q != z)
    def _():
        for d in range(N):
            pltpu.make_async_remote_copy(
                src_ref=scol.at[z], dst_ref=srow.at[d],
                send_sem=row_send.at[0], recv_sem=row_recv.at[d],
                device_id={"tensor": lax.rem(q + 1, N), "dp": q}, device_id_type=MESH,
            ).wait_recv()

    @pl.when(q == z)
    def _():
        srow[...] = scol[...]

    width = OWN * RANK
    col_hi, col_lo = split(scol[...].reshape(N * DOCS_DEV, width))
    row_t = srow[...].reshape(N * DOCS_DEV, width).T
    row_hi, row_lo = split(row_t)
    lhs = jnp.concatenate([row_hi, row_lo, row_hi], axis=1)
    rhs = jnp.concatenate([col_hi, col_hi, col_lo], axis=0)
    fisher_ref[...] = jnp.dot(lhs, rhs, preferred_element_type=F32) * (1.0 / (N * DOCS_DEV))
    for d in range(N - 1):
        row_copy(d).wait_send()
        col_copy(d).wait_send()


def per_device_fused(activations, out_grads, proj_in, proj_out, document_ids):
    tokens, ff = activations.shape
    width = out_grads.shape[1]
    blocks = tokens // TB
    ids = document_ids.reshape(blocks, 1, TB)
    vmem = pl.BlockSpec(memory_space=pltpu.VMEM)
    hbm = pl.BlockSpec(memory_space=pl.ANY)
    cols = OWN * RANK
    dma = pltpu.SemaphoreType.DMA
    return pl.pallas_call(
        kernel,
        out_shape=(
            jax.ShapeDtypeStruct((DOCS_DEV, cols), F32),
            jax.ShapeDtypeStruct((cols, cols), F32),
        ),
        in_specs=[hbm, hbm, vmem, vmem, vmem],
        out_specs=(vmem, vmem),
        scratch_shapes=[
            pltpu.VMEM((blocks, TB, ff), BF16),
            pltpu.VMEM((blocks, TB, width), BF16),
            pltpu.VMEM((blocks, 2 * RANK, TB), F32),
            pltpu.VMEM((blocks, 2 * RANK, TB), F32),
            pltpu.VMEM((blocks, RANK + OWN, TB), F32),
            pltpu.VMEM((blocks, RANK + OWN, TB), F32),
            pltpu.VMEM((blocks, RANK + OWN, TB), F32),
            pltpu.VMEM((2 * OWN * DOCS_DEV, 2 * RANK), F32),
            pltpu.VMEM((N, DOCS_DEV, cols), F32),
            pltpu.VMEM((N, DOCS_DEV, cols), F32),
            dma((blocks,)), dma((blocks,)), dma((blocks,)), dma((blocks,)),
            dma((blocks,)), dma((blocks,)),
            dma((N - 1,)), dma((N - 1,)), dma((N - 1,)), dma((N,)),
        ],
        compiler_params=pltpu.CompilerParams(
            collective_id=0, has_side_effects=True, vmem_limit_bytes=56 * 1024 * 1024
        ),
        cost_estimate=pl.CostEstimate(
            flops=2 * tokens * (ff + width) * RANK,
            bytes_accessed=2 * tokens * (ff + width), transcendentals=0,
        ),
    )(activations, out_grads, proj_in, proj_out, ids)


def solution(mesh):
    fits = mesh.shape["tensor"] == N and mesh.shape["dp"] == N
    return jax.shard_map(
        per_device_fused if fits else per_device_general,
        mesh=mesh,
        in_specs=(
            P(("groups", "dp"), "tensor"),
            P(("groups", "dp"), "tensor"),
            P(("groups", "tensor"), None),
            P(("groups", "tensor"), None),
            P(("groups", "dp"), None),
        ),
        out_specs=(P(("groups", "dp"), "tensor"), P(("groups", "dp"), "tensor")),
        check_vma=False,
    )
```

time: 109 us -> 46.9 us (0.43)
  Pallas kernels: 0 us -> 38.4 us
  waiting for transfers between devices: 35.9 us -> 0 us
  blocking collectives: 28.5 us -> 0 us
  matrix products: 27 us -> 0 us
  between operations: 14.1 us -> 0.64 us
  local copies, waits for them, and re-layouts: 0.99 us -> 7.52 us
  other arithmetic: 2.2 us -> 0 us
    pallas_call x0 -> x1, Pallas kernels: none -> 38.4 us  [per_device_fused(): pl.pallas_call(kernel, out_shape=(jax.ShapeDtypeStruct((DOCS_DEV, cols),...]
    psum x1 -> x0, waiting for transfers between devices: 35.9 us -> none  [per_device(): in_proj, out_proj = lax.psum((in_part, out_part), 'tensor')]
    all_gather x2 -> x0, blocking collectives: 28.5 us -> none  [the longest x1 14.9 us: per_device(): lax.all_gather(full_sketch, 'dp', axis=0, tiled=True)]
    dot_general x4 -> x0, matrix products: 27 us -> none  [the longest x1 14.7 us: per_device(): in_part = jnp.dot(activations, proj_in, preferred_element_type=jnp.float32)]
    unnamed x10 -> x4, local copies, waits for them, and re-layouts: 0.98 us -> 7.52 us
    mul x1 -> x0, other arithmetic: 2.06 us -> none  [sketch_terms(): out_proj[:, :, None] * in_proj[:, None, :]]
  transfers between devices with their start and end apart: 1 -> 0, of which waited for: 1 -> 0; matrix products, arithmetic and copies ran while one was open for 0% -> 0% of each run, Pallas kernels for 0% -> 0%
where the time goes in v1:
time: 46.9 us; the launch traced here: 46.6 us
  Pallas kernels  38.4 us (82%)
  local copies, waits for them, and re-layouts  7.52 us (16%)
  between operations  0.64 us (1%)
    pallas_call x1, Pallas kernels, per_device_fused(): pl.pallas_call(kernel, out_shape=(jax.ShapeDtypeStruct((DOCS_DEV, cols),...  38.4 us
    unnamed x4, local copies, waits for them, and re-layouts  7.52 us

profile of v1, /device:TPU:0, one launch (start us, length us, event | category | flops | bytes accessed | tf_op | source)
XLA Modules:
  0.0 46.6 jit_solution(11167145848850179332)
XLA Ops:
  0.6 1.9 %copy.8.pout_ref = bf16[2048,32]{1,0:T(8,128)(2,1)} copy(bf16[2048,32]{0,1:T(8,128)(2,1)} %param.8) | data formatting | bytes 262144 | tf_op args[3]
  2.6 2.5 %copy.7.pin_ref = bf16[7168,32]{1,0:T(8,128)(2,1)} copy(bf16[7168,32]{0,1:T(8,128)(2,1)} %param.7) | data formatting | bytes 917504 | tf_op args[2]
  5.1 38.4 %shard_map.68 = (f32[32,256]{1,0:T(8,128)}, f32[256,256]{1,0:T(8,128)}) custom-call(bf16[2048,7168]{1,0:T(8,128)(2,1)} %act_hbm.1, bf16[2048,2048]{1,0:T(8,128)(2,1)} %grad_hbm.1, bf16[7168,32]{1,0:T(8,128)(2,1)} %copy.7.pin_ref, bf16[2048,32]{1,0:T(8,128)(2,1)} %copy.8.pout_ref, s32[8,1,256]{2,1,0:T(1,128)} %bitcast.1), custom_call_target="tpu_custom_call" | custom-call | flops 1207959552 | bytes 37748736 | tf_op jit(solution)/shard_map/pallas_call | solution.py:227
  43.6 1.4 %copy.11 = f32[32,256]{1,0:T(8,128)} copy(f32[32,256]{1,0:T(8,128)} %get-tuple-element.4) | data formatting | bytes 65536
  44.9 1.7 %copy.12 = f32[256,256]{1,0:T(8,128)} copy(f32[256,256]{1,0:T(8,128)} %get-tuple-element.5) | data formatting | bytes 524288

commit v2 on v1

--- a/solution.py
+++ b/solution.py
@@ -55,11 +55,15 @@
     return hi, (x - hi.astype(F32)).astype(BF16)
 
 
+def across(a, b):
+    return lax.dot_general(a, b, (((1,), (1,)), ((), ())), preferred_element_type=F32)
+
+
 def kernel(
-    act_hbm, grad_hbm, pin_ref, pout_ref, ids_ref, sketch_ref, fisher_ref,
-    act, grad, part, sib, mine, send, recv, acc, scol, srow,
-    act_sem, grad_sem, sib_send, sib_recv, x_send, x_recv,
-    col_send, col_recv, row_send, row_recv,
+    act_hbm, grad_hbm, pin_hbm, pout_hbm, ids_ref, scol, srow,
+    act, grad, pin_ref, pout_ref, part, sib, mine, send, recv, acc, count, own,
+    act_sem, grad_sem, proj_sem, sib_send, sib_recv, x_send, x_recv,
+    own_sem, col_send, col_recv, row_send, row_recv,
 ):
     q = lax.axis_index("tensor")
     z = lax.axis_index("dp")
@@ -70,8 +74,8 @@
     def load(b):
         rows = pl.ds(pl.multiple_of(b * TB, TB), TB)
         return (
+            pltpu.make_async_copy(grad_hbm.at[rows], grad.at[b], grad_sem.at[b]),
             pltpu.make_async_copy(act_hbm.at[rows], act.at[b], act_sem.at[b]),
-            pltpu.make_async_copy(grad_hbm.at[rows], grad.at[b], grad_sem.at[b]),
         )
 
     def to_core(b):
@@ -85,6 +89,13 @@
             src_ref=send.at[b], dst_ref=recv.at[b], send_sem=x_send.at[b], recv_sem=x_recv.at[b],
             device_id={"tensor": chip_peer}, device_id_type=MESH,
         )
+
+    proj_copies = (
+        pltpu.make_async_copy(pout_hbm, pout_ref, proj_sem.at[0]),
+        pltpu.make_async_copy(pin_hbm, pin_ref, proj_sem.at[1]),
+    )
+    for copy in proj_copies:
+        copy.start()
 
     @pl.loop(0, blocks)
     def _(b):
@@ -103,20 +114,19 @@
 
     acc[...] = jnp.zeros_like(acc)
     docs = lax.broadcasted_iota(jnp.int32, (DOCS_DEV, 1), 0)
-    length = jnp.zeros((DOCS_DEV, 1), F32)
-    for b in range(blocks):
-        same = (ids_ref[b] == docs).astype(F32)
-        length = length + jnp.sum(same, axis=1, keepdims=True)
-    scale = lax.rsqrt(length)
-    pl.semaphore_wait(barrier, N * N - 1)
+    count[...] = jnp.zeros_like(count)
 
     def project(b):
-        for copy in load(b):
-            copy.wait()
-        p_in = jnp.dot(act[b], pin_ref[...], preferred_element_type=F32)
-        p_out = jnp.dot(grad[b], pout_ref[...], preferred_element_type=F32)
-        part[b, pl.ds(0, RANK)] = p_in.T
-        part[b, pl.ds(RANK, RANK)] = p_out.T
+        grad_copy, act_copy = load(b)
+        grad_copy.wait()
+        act_copy.wait()
+        part[b, pl.ds(RANK, RANK)] = across(pout_ref[...], grad[b])
+        part[b, pl.ds(0, RANK)] = across(pin_ref[...], act[b])
+
+        @pl.when(b == 0)
+        def _():
+            pl.semaphore_wait(barrier, N * N - 1)
+
         to_core(b).start()
 
     def chip_sum(b):
@@ -136,83 +146,77 @@
         in_hi, in_lo = split(total[:RANK])
         rhs = jnp.concatenate([in_hi, in_lo], axis=0)
         same = (ids_ref[b] == docs).astype(F32)
+        count[...] += same
         out = total[RANK:]
         out_hi = out.astype(BF16).astype(F32)
         out_lo = out - out_hi
         rows = [same * o[i : i + 1] for o in (out_hi, out_lo) for i in range(OWN)]
         lhs = jnp.concatenate(rows, axis=0).astype(BF16)
-        acc[...] += lax.dot_general(
-            lhs, rhs, (((1,), (1,)), ((), ())), preferred_element_type=F32
-        )
-
-    project(0)
-    project(1)
-    chip_sum(0)
-
-    @pl.loop(2, blocks)
+        acc[...] += across(lhs, rhs)
+
+    for copy in proj_copies:
+        copy.wait()
+
+    @pl.loop(0, blocks + 2)
     def _(b):
-        project(b)
-        chip_sum(b - 1)
-        sketch(b - 2)
-
-    chip_sum(blocks - 1)
-    sketch(blocks - 2)
-    sketch(blocks - 1)
-
+        pl.when(b < blocks)(lambda: project(b))
+        pl.when((b > 0) & (b <= blocks))(lambda: chip_sum(b - 1))
+        pl.when(b > 1)(lambda: sketch(b - 2))
+
+    scale = lax.rsqrt(jnp.sum(count[...], axis=1, keepdims=True))
     half = OWN * DOCS_DEV
     for i in range(OWN):
         hi = acc[pl.ds(i * DOCS_DEV, DOCS_DEV)]
         lo = acc[pl.ds(half + i * DOCS_DEV, DOCS_DEV)]
         both = hi + lo
         piece = (both[:, :RANK] + both[:, RANK:]) * scale
-        scol[z, :, pl.ds(i * RANK, RANK)] = piece
-
-    def col_copy(d):
-        return pltpu.make_async_remote_copy(
-            src_ref=scol.at[z], dst_ref=scol.at[z], send_sem=col_send.at[d], recv_sem=col_recv.at[d],
+        own[:, pl.ds(i * RANK, RANK)] = piece
+
+    def keep():
+        return pltpu.make_async_copy(own, scol.at[z], own_sem)
+
+    def col_copy(d, slot):
+        return pltpu.make_async_remote_copy(
+            src_ref=own, dst_ref=scol.at[slot], send_sem=col_send.at[d], recv_sem=col_recv.at[d],
             device_id={"dp": lax.rem(z + d + 1, N)}, device_id_type=MESH,
         )
 
-    def row_copy(d):
-        return pltpu.make_async_remote_copy(
-            src_ref=scol.at[z], dst_ref=srow.at[z], send_sem=row_send.at[d], recv_sem=row_recv.at[z],
+    def row_copy(d, slot):
+        return pltpu.make_async_remote_copy(
+            src_ref=own, dst_ref=srow.at[slot], send_sem=row_send.at[d], recv_sem=row_recv.at[slot],
             device_id={"tensor": lax.rem(q + d + 1, N), "dp": q}, device_id_type=MESH,
         )
 
     for d in range(N - 1):
-        row_copy(d).start()
-        col_copy(d).start()
-    sketch_ref[...] = scol[z]
+        row_copy(d, z).start()
+        col_copy(d, z).start()
+    keep().start()
+    keep().wait()
     for d in range(N - 1):
-        pltpu.make_async_remote_copy(
-            src_ref=scol.at[z], dst_ref=scol.at[lax.rem(z + N - d - 1, N)],
-            send_sem=col_send.at[d], recv_sem=col_recv.at[d],
-            device_id={"dp": lax.rem(z + d + 1, N)}, device_id_type=MESH,
-        ).wait_recv()
+        col_copy(d, lax.rem(z + N - d - 1, N)).wait_recv()
 
     @pl.when(q != z)
     def _():
         for d in range(N):
-            pltpu.make_async_remote_copy(
-                src_ref=scol.at[z], dst_ref=srow.at[d],
-                send_sem=row_send.at[0], recv_sem=row_recv.at[d],
-                device_id={"tensor": lax.rem(q + 1, N), "dp": q}, device_id_type=MESH,
-            ).wait_recv()
-
-    @pl.when(q == z)
-    def _():
-        srow[...] = scol[...]
-
-    width = OWN * RANK
-    col_hi, col_lo = split(scol[...].reshape(N * DOCS_DEV, width))
-    row_t = srow[...].reshape(N * DOCS_DEV, width).T
-    row_hi, row_lo = split(row_t)
+            row_copy(0, d).wait_recv()
+
+    for d in range(N - 1):
+        row_copy(d, z).wait_send()
+        col_copy(d, z).wait_send()
+
+
+def fisher_kernel(col_ref, row_ref, sketch_ref, fisher_ref):
+    q = lax.axis_index("tensor")
+    z = lax.axis_index("dp")
+    docs, width = N * DOCS_DEV, OWN * RANK
+    sketch_ref[...] = col_ref[z]
+    cols = col_ref[...].reshape(docs, width)
+    rows = jnp.where(q == z, cols, row_ref[...].reshape(docs, width))
+    col_hi, col_lo = split(cols)
+    row_hi, row_lo = split(rows.T)
     lhs = jnp.concatenate([row_hi, row_lo, row_hi], axis=1)
     rhs = jnp.concatenate([col_hi, col_hi, col_lo], axis=0)
-    fisher_ref[...] = jnp.dot(lhs, rhs, preferred_element_type=F32) * (1.0 / (N * DOCS_DEV))
-    for d in range(N - 1):
-        row_copy(d).wait_send()
-        col_copy(d).wait_send()
+    fisher_ref[...] = jnp.dot(lhs, rhs, preferred_element_type=F32) * (1.0 / docs)
 
 
 def per_device_fused(activations, out_grads, proj_in, proj_out, document_ids):
@@ -224,37 +228,46 @@
     hbm = pl.BlockSpec(memory_space=pl.ANY)
     cols = OWN * RANK
     dma = pltpu.SemaphoreType.DMA
-    return pl.pallas_call(
+    gathered = jax.ShapeDtypeStruct((N, DOCS_DEV, cols), F32)
+    scol, srow = pl.pallas_call(
         kernel,
-        out_shape=(
-            jax.ShapeDtypeStruct((DOCS_DEV, cols), F32),
-            jax.ShapeDtypeStruct((cols, cols), F32),
-        ),
-        in_specs=[hbm, hbm, vmem, vmem, vmem],
-        out_specs=(vmem, vmem),
+        out_shape=(gathered, gathered),
+        in_specs=[hbm, hbm, hbm, hbm, vmem],
+        out_specs=(hbm, hbm),
         scratch_shapes=[
             pltpu.VMEM((blocks, TB, ff), BF16),
             pltpu.VMEM((blocks, TB, width), BF16),
+            pltpu.VMEM((RANK, ff), BF16),
+            pltpu.VMEM((RANK, width), BF16),
             pltpu.VMEM((blocks, 2 * RANK, TB), F32),
             pltpu.VMEM((blocks, 2 * RANK, TB), F32),
             pltpu.VMEM((blocks, RANK + OWN, TB), F32),
             pltpu.VMEM((blocks, RANK + OWN, TB), F32),
             pltpu.VMEM((blocks, RANK + OWN, TB), F32),
             pltpu.VMEM((2 * OWN * DOCS_DEV, 2 * RANK), F32),
-            pltpu.VMEM((N, DOCS_DEV, cols), F32),
-            pltpu.VMEM((N, DOCS_DEV, cols), F32),
-            dma((blocks,)), dma((blocks,)), dma((blocks,)), dma((blocks,)),
+            pltpu.VMEM((DOCS_DEV, TB), F32),
+            pltpu.VMEM((DOCS_DEV, cols), F32),
+            dma((blocks,)), dma((blocks,)), dma((2,)), dma((blocks,)), dma((blocks,)),
             dma((blocks,)), dma((blocks,)),
-            dma((N - 1,)), dma((N - 1,)), dma((N - 1,)), dma((N,)),
+            dma, dma((N - 1,)), dma((N - 1,)), dma((N - 1,)), dma((N,)),
         ],
         compiler_params=pltpu.CompilerParams(
-            collective_id=0, has_side_effects=True, vmem_limit_bytes=56 * 1024 * 1024
+            collective_id=0, has_side_effects=True, vmem_limit_bytes=58 * 1024 * 1024
         ),
         cost_estimate=pl.CostEstimate(
             flops=2 * tokens * (ff + width) * RANK,
             bytes_accessed=2 * tokens * (ff + width), transcendentals=0,
         ),
-    )(activations, out_grads, proj_in, proj_out, ids)
+    )(activations, out_grads, proj_in.T, proj_out.T, ids)
+    return pl.pallas_call(
+        fisher_kernel,
+        out_shape=(
+            jax.ShapeDtypeStruct((DOCS_DEV, cols), F32),
+            jax.ShapeDtypeStruct((cols, cols), F32),
+        ),
+        in_specs=[vmem, vmem],
+        out_specs=(vmem, vmem),
+    )(scol, srow)
 
 
 def solution(mesh):

time: 46.9 us -> 39.2 us (0.84)
  local copies, waits for them, and re-layouts: 7.52 us -> 0 us
    unnamed x4 -> x0, local copies, waits for them, and re-layouts: 7.52 us -> none
    pallas_call x1 -> x2, Pallas kernels: 38.4 us -> 38.3 us  [the longest x1 36.4 us: per_device_fused(): pl.pallas_call(kernel, out_shape=(gathered, gathered), in_specs=[hbm, hbm...]
where the time goes in v2:
time: 39.2 us; the launch traced here: 39 us
  Pallas kernels  38.3 us (98%)
  between operations  0.64 us (2%)
    pallas_call x1, Pallas kernels, per_device_fused(): pl.pallas_call(kernel, out_shape=(gathered, gathered), in_specs=[hbm, hbm...  36.4 us
    pallas_call x1, Pallas kernels, per_device_fused(): pl.pallas_call(fisher_kernel, out_shape=(jax.ShapeDtypeStruct((DOCS_DEV,...  1.96 us

profile of v2, /device:TPU:0, one launch (start us, length us, event | category | flops | bytes accessed | tf_op | source)
XLA Modules:
  0.0 39.0 jit_solution(307350615033151003)
XLA Ops:
  0.6 36.4 %shard_map.68 = (f32[4,32,256]{2,1,0:T(8,128)}, f32[4,32,256]{2,1,0:T(8,128)}) custom-call(bf16[2048,7168]{1,0:T(8,128)(2,1)} %act_hbm.1, bf16[2048,2048]{1,0:T(8,128)(2,1)} %grad_hbm.1, bf16[32,7168]{1,0:T(8,128)(2,1)} %bitcast.3, bf16[32,2048]{1,0:T(8,128)(2,1)} %bitcast.4, s32[8,1,256]{2,1,0:T(1,128)} %bitcast.5), custom_call_target="tpu_custom_call" | custom-call | flops 1207959552 | bytes 37748736 | tf_op jit(solution)/shard_map/pallas_call | solution.py:232
  37.0 2.0 %shard_map.69 = (f32[32,256]{1,0:T(8,128)}, f32[256,256]{1,0:T(8,128)}) custom-call(f32[4,32,256]{2,1,0:T(8,128)} %get-tuple-element.4.col_ref, f32[4,32,256]{2,1,0:T(8,128)} %get-tuple-element.5.row_ref), custom_call_target="tpu_custom_call" | custom-call | tf_op jit(solution)/shard_map/pallas_call | solution.py:262

commit v3 on v2

--- a/solution.py
+++ b/solution.py
@@ -45,7 +45,9 @@
 
 
 N = 4
-TB = 256
+TB = 512
+MOST = 128
+EARLY = 8
 RANK = 32
 OWN = RANK // N
 
@@ -157,52 +159,61 @@
     for copy in proj_copies:
         copy.wait()
 
+    parts = ((0, EARLY), (EARLY, DOCS_DEV - EARLY))
+
+    def finish(p):
+        first, size = parts[p]
+        half = OWN * DOCS_DEV
+        scale = lax.rsqrt(jnp.sum(count[pl.ds(first, size)], axis=1, keepdims=True))
+        for i in range(OWN):
+            hi = acc[pl.ds(i * DOCS_DEV + first, size)]
+            lo = acc[pl.ds(half + i * DOCS_DEV + first, size)]
+            both = hi + lo
+            piece = (both[:, :RANK] + both[:, RANK:]) * scale
+            own[pl.ds(first, size), pl.ds(i * RANK, RANK)] = piece
+        for d in range(N - 1):
+            col_copy(p, (1, 0, 2)[d], z).start()
+            row_copy(p, d, z).start()
+
+    def col_copy(p, d, slot):
+        return pltpu.make_async_remote_copy(
+            src_ref=own.at[pl.ds(*parts[p])], dst_ref=scol.at[slot, pl.ds(*parts[p])],
+            send_sem=col_send.at[p, d], recv_sem=col_recv.at[p, d],
+            device_id={"dp": lax.rem(z + d + 1, N)}, device_id_type=MESH,
+        )
+
+    def row_copy(p, d, slot):
+        return pltpu.make_async_remote_copy(
+            src_ref=own.at[pl.ds(*parts[p])], dst_ref=srow.at[slot, pl.ds(*parts[p])],
+            send_sem=row_send.at[p, d], recv_sem=row_recv.at[p, slot],
+            device_id={"tensor": lax.rem(q + d + 1, N), "dp": q}, device_id_type=MESH,
+        )
+
     @pl.loop(0, blocks + 2)
     def _(b):
         pl.when(b < blocks)(lambda: project(b))
         pl.when((b > 0) & (b <= blocks))(lambda: chip_sum(b - 1))
         pl.when(b > 1)(lambda: sketch(b - 2))
-
-    scale = lax.rsqrt(jnp.sum(count[...], axis=1, keepdims=True))
-    half = OWN * DOCS_DEV
-    for i in range(OWN):
-        hi = acc[pl.ds(i * DOCS_DEV, DOCS_DEV)]
-        lo = acc[pl.ds(half + i * DOCS_DEV, DOCS_DEV)]
-        both = hi + lo
-        piece = (both[:, :RANK] + both[:, RANK:]) * scale
-        own[:, pl.ds(i * RANK, RANK)] = piece
-
-    def keep():
-        return pltpu.make_async_copy(own, scol.at[z], own_sem)
-
-    def col_copy(d, slot):
-        return pltpu.make_async_remote_copy(
-            src_ref=own, dst_ref=scol.at[slot], send_sem=col_send.at[d], recv_sem=col_recv.at[d],
-            device_id={"dp": lax.rem(z + d + 1, N)}, device_id_type=MESH,
-        )
-
-    def row_copy(d, slot):
-        return pltpu.make_async_remote_copy(
-            src_ref=own, dst_ref=srow.at[slot], send_sem=row_send.at[d], recv_sem=row_recv.at[slot],
-            device_id={"tensor": lax.rem(q + d + 1, N), "dp": q}, device_id_type=MESH,
-        )
-
-    for d in range(N - 1):
-        row_copy(d, z).start()
-        col_copy(d, z).start()
-    keep().start()
-    keep().wait()
-    for d in range(N - 1):
-        col_copy(d, lax.rem(z + N - d - 1, N)).wait_recv()
+        pl.when(b == EARLY * MOST // TB + 1)(lambda: finish(0))
+
+    finish(1)
+    keep = pltpu.make_async_copy(own, scol.at[z], own_sem)
+    keep.start()
+    keep.wait()
+    for p in range(2):
+        for d in range(N - 1):
+            col_copy(p, d, lax.rem(z + N - d - 1, N)).wait_recv()
 
     @pl.when(q != z)
     def _():
-        for d in range(N):
-            row_copy(0, d).wait_recv()
-
-    for d in range(N - 1):
-        row_copy(d, z).wait_send()
-        col_copy(d, z).wait_send()
+        for p in range(2):
+            for d in range(N):
+                row_copy(p, 0, d).wait_recv()
+
+    for p in range(2):
+        for d in range(N - 1):
+            row_copy(p, d, z).wait_send()
+            col_copy(p, d, z).wait_send()
 
 
 def fisher_kernel(col_ref, row_ref, sketch_ref, fisher_ref):
@@ -249,7 +260,7 @@
             pltpu.VMEM((DOCS_DEV, cols), F32),
             dma((blocks,)), dma((blocks,)), dma((2,)), dma((blocks,)), dma((blocks,)),
             dma((blocks,)), dma((blocks,)),
-            dma, dma((N - 1,)), dma((N - 1,)), dma((N - 1,)), dma((N,)),
+            dma, dma((2, N - 1)), dma((2, N - 1)), dma((2, N - 1)), dma((2, N)),
         ],
         compiler_params=pltpu.CompilerParams(
             collective_id=0, has_side_effects=True, vmem_limit_bytes=58 * 1024 * 1024

time: 39.2 us -> 35.3 us (0.901)
  Pallas kernels: 38.3 us -> 34.4 us
    pallas_call x1, Pallas kernels: 36.4 us -> 32.5 us  [per_device_fused(): pl.pallas_call(kernel, out_shape=(gathered, gathered), in_specs=[hbm, hbm...]
where the time goes in v3:
time: 35.3 us; the launch traced here: 35.1 us
  Pallas kernels  34.4 us (97%)
  between operations  0.64 us (2%)
    pallas_call x1, Pallas kernels, per_device_fused(): pl.pallas_call(kernel, out_shape=(gathered, gathered), in_specs=[hbm, hbm...  32.5 us
    pallas_call x1, Pallas kernels, per_device_fused(): pl.pallas_call(fisher_kernel, out_shape=(jax.ShapeDtypeStruct((DOCS_DEV,...  1.96 us

profile of v3, /device:TPU:0, one launch (start us, length us, event | category | flops | bytes accessed | tf_op | source)
XLA Modules:
  0.0 35.1 jit_solution(713802506777402306)
XLA Ops:
  0.6 32.5 %shard_map.68 = (f32[4,32,256]{2,1,0:T(8,128)}, f32[4,32,256]{2,1,0:T(8,128)}) custom-call(bf16[2048,7168]{1,0:T(8,128)(2,1)} %act_hbm.1, bf16[2048,2048]{1,0:T(8,128)(2,1)} %grad_hbm.1, bf16[32,7168]{1,0:T(8,128)(2,1)} %bitcast.3, bf16[32,2048]{1,0:T(8,128)(2,1)} %bitcast.4, s32[4,1,512]{2,1,0:T(1,128)} %bitcast.5), custom_call_target="tpu_custom_call" | custom-call | flops 1207959552 | bytes 37748736 | tf_op jit(solution)/shard_map/pallas_call | solution.py:243
  33.1 2.0 %shard_map.69 = (f32[32,256]{1,0:T(8,128)}, f32[256,256]{1,0:T(8,128)}) custom-call(f32[4,32,256]{2,1,0:T(8,128)} %get-tuple-element.4.col_ref, f32[4,32,256]{2,1,0:T(8,128)} %get-tuple-element.5.row_ref), custom_call_target="tpu_custom_call" | custom-call | tf_op jit(solution)/shard_map/pallas_call | solution.py:273

commit v4 on v3

--- a/solution.py
+++ b/solution.py
@@ -46,6 +46,7 @@
 
 N = 4
 TB = 512
+SUB = 256
 MOST = 128
 EARLY = 8
 RANK = 32
@@ -69,15 +70,16 @@
 ):
     q = lax.axis_index("tensor")
     z = lax.axis_index("dp")
-    blocks = act.shape[0]
+    pieces = act.shape[0]
+    blocks = part.shape[0]
     core_peer = q + 1 - 2 * lax.rem(q, 2)
     chip_peer = lax.rem(q + 2, N)
 
-    def load(b):
-        rows = pl.ds(pl.multiple_of(b * TB, TB), TB)
+    def load(c):
+        rows = pl.ds(pl.multiple_of(c * SUB, SUB), SUB)
         return (
-            pltpu.make_async_copy(grad_hbm.at[rows], grad.at[b], grad_sem.at[b]),
-            pltpu.make_async_copy(act_hbm.at[rows], act.at[b], act_sem.at[b]),
+            pltpu.make_async_copy(grad_hbm.at[rows], grad.at[c], grad_sem.at[c]),
+            pltpu.make_async_copy(act_hbm.at[rows], act.at[c], act_sem.at[c]),
         )
 
     def to_core(b):
@@ -99,9 +101,9 @@
     for copy in proj_copies:
         copy.start()
 
-    @pl.loop(0, blocks)
-    def _(b):
-        for copy in load(b):
+    @pl.loop(0, pieces)
+    def _(c):
+        for copy in load(c):
             copy.start()
 
     barrier = pltpu.get_barrier_semaphore()
@@ -119,11 +121,14 @@
     count[...] = jnp.zeros_like(count)
 
     def project(b):
-        grad_copy, act_copy = load(b)
-        grad_copy.wait()
-        act_copy.wait()
-        part[b, pl.ds(RANK, RANK)] = across(pout_ref[...], grad[b])
-        part[b, pl.ds(0, RANK)] = across(pin_ref[...], act[b])
+        @pl.loop(0, TB // SUB)
+        def _(h):
+            c = b * (TB // SUB) + h
+            at = pl.ds(pl.multiple_of(h * SUB, SUB), SUB)
+            for copy in load(c):
+                copy.wait()
+            part[b, pl.ds(RANK, RANK), at] = across(pout_ref[...], grad[c])
+            part[b, pl.ds(0, RANK), at] = across(pin_ref[...], act[c])
 
         @pl.when(b == 0)
         def _():
@@ -246,8 +251,8 @@
         in_specs=[hbm, hbm, hbm, hbm, vmem],
         out_specs=(hbm, hbm),
         scratch_shapes=[
-            pltpu.VMEM((blocks, TB, ff), BF16),
-            pltpu.VMEM((blocks, TB, width), BF16),
+            pltpu.VMEM((tokens // SUB, SUB, ff), BF16),
+            pltpu.VMEM((tokens // SUB, SUB, width), BF16),
             pltpu.VMEM((RANK, ff), BF16),
             pltpu.VMEM((RANK, width), BF16),
             pltpu.VMEM((blocks, 2 * RANK, TB), F32),
@@ -258,7 +263,7 @@
             pltpu.VMEM((2 * OWN * DOCS_DEV, 2 * RANK), F32),
             pltpu.VMEM((DOCS_DEV, TB), F32),
             pltpu.VMEM((DOCS_DEV, cols), F32),
-            dma((blocks,)), dma((blocks,)), dma((2,)), dma((blocks,)), dma((blocks,)),
+            dma((tokens // SUB,)), dma((tokens // SUB,)), dma((2,)), dma((blocks,)), dma((blocks,)),
             dma((blocks,)), dma((blocks,)),
             dma, dma((2, N - 1)), dma((2, N - 1)), dma((2, N - 1)), dma((2, N)),
         ],

time: 35.3 us -> 34 us (0.963)
  Pallas kernels: 34.4 us -> 33 us
    pallas_call x1, Pallas kernels: 32.5 us -> 31.1 us  [per_device_fused(): pl.pallas_call(kernel, out_shape=(gathered, gathered), in_specs=[hbm, hbm...]
where the time goes in v4:
time: 34 us; the launch traced here: 33.7 us
  Pallas kernels  33 us (97%)
  between operations  0.64 us (2%)
    pallas_call x1, Pallas kernels, per_device_fused(): pl.pallas_call(kernel, out_shape=(gathered, gathered), in_specs=[hbm, hbm...  31.1 us
    pallas_call x1, Pallas kernels, per_device_fused(): pl.pallas_call(fisher_kernel, out_shape=(jax.ShapeDtypeStruct((DOCS_DEV,...  1.96 us

profile of v4, /device:TPU:0, one launch (start us, length us, event | category | flops | bytes accessed | tf_op | source)
XLA Modules:
  0.0 33.7 jit_solution(5978287178398311073)
XLA Ops:
  0.6 31.1 %shard_map.68 = (f32[4,32,256]{2,1,0:T(8,128)}, f32[4,32,256]{2,1,0:T(8,128)}) custom-call(bf16[2048,7168]{1,0:T(8,128)(2,1)} %act_hbm.1, bf16[2048,2048]{1,0:T(8,128)(2,1)} %grad_hbm.1, bf16[32,7168]{1,0:T(8,128)(2,1)} %bitcast.3, bf16[32,2048]{1,0:T(8,128)(2,1)} %bitcast.4, s32[4,1,512]{2,1,0:T(1,128)} %bitcast.5), custom_call_target="tpu_custom_call" | custom-call | flops 1207959552 | bytes 37748736 | tf_op jit(solution)/shard_map/pallas_call | solution.py:248
  31.7 2.0 %shard_map.69 = (f32[32,256]{1,0:T(8,128)}, f32[256,256]{1,0:T(8,128)}) custom-call(f32[4,32,256]{2,1,0:T(8,128)} %get-tuple-element.4.col_ref, f32[4,32,256]{2,1,0:T(8,128)} %get-tuple-element.5.row_ref), custom_call_target="tpu_custom_call" | custom-call | tf_op jit(solution)/shard_map/pallas_call | solution.py:278
